TPU v7x, 256 devices: a whole 4x4x8 slice. The times are simulated.
256 devices in a mesh: seq: 32 (over z_lo, y, core), head: 8 (over z_hi, x).
Axes of the slice: x: 4, y: 4, z: 8 (z_hi: 2, z_lo: 4; z = z_hi * 4 + z_lo), core: 2. Of those that a mesh axis runs over, the one named last changes fastest.
Arguments:
- queries: bfloat16 [32768, 8192], P(('seq', 'head')), may hold values from -17 to 17
- keys: bfloat16 [32768, 1024], P(('seq', 'head')), may hold values from -17 to 17
- values: bfloat16 [32768, 1024], P(('seq', 'head')), may hold values from -6 to 6
- lengths: int32 [64], replicated, may hold values from 1 to 2048, 32768 in all
Outputs:
- attended: bfloat16 [32768, 8192], P(('seq', 'head'))
Inputs may be any that keep to these rules, and one draw needn't show every extreme that they name: document lengths sum to 32768; the longest is exactly 2048.
All inputs are finite; a program needn't handle non-finite values.
Results may differ from a plain program's by a relative error of at most 0.0044.
Values may be sent and summed in bfloat16 or wider, within the bound.
A program may use at most 128 MiB of HBM per device.

v0:
```python
import math

import jax
import jax.numpy as jnp
from jax import lax
from jax.sharding import PartitionSpec as P

H = 64
KVH = 8
DH = 128
REACH = 2


def shifted(value, axis, steps):
    count = lax.axis_size(axis)
    leading, last = (max(0, -steps), min(count, count - steps))
    return lax.ppermute(value, axis, [(source, source + steps) for source in range(leading, last)])


def doc_of(places, ends):
    return jnp.sum((ends[None, :] <= places[:, None]).astype(jnp.int32), axis=1)


def earlier_blocks(paired):
    blocks = []
    for step in range(1, REACH + 1):
        blocks.append(shifted(paired, "seq", step))
    return blocks


def attend(query_heads, query_pos, blocks, ends):
    count = query_heads.shape[0]
    kv_local = query_heads.shape[1]
    group = query_heads.shape[2]
    width_head = query_heads.shape[3]
    scale = 1.0 / width_head**0.5
    rows_all = group * count
    width = math.gcd(rows_all, 1024)
    parts = rows_all // width
    query_rows = jnp.transpose(query_heads, (1, 2, 0, 3)).reshape(
        kv_local * parts, width, width_head
    )
    row_pos = jnp.tile(query_pos, group).reshape(parts, width)
    row_doc = jnp.tile(doc_of(query_pos, ends), group).reshape(parts, width)
    prepared = [(paired, key_pos, doc_of(key_pos, ends)) for paired, key_pos in blocks]

    def one_item(item):
        head = item // parts
        part = item % parts
        query_now = lax.dynamic_index_in_dim(query_rows, item, 0, keepdims=False)
        pos_now = lax.dynamic_index_in_dim(row_pos, part, 0, keepdims=False)
        doc_now = lax.dynamic_index_in_dim(row_doc, part, 0, keepdims=False)
        carry = (
            jnp.full((width,), -1e30, jnp.float32),
            jnp.zeros((width,), jnp.float32),
            jnp.zeros((width, width_head), jnp.float32),
        )
        for paired, key_pos, key_doc in prepared:
            pair_head = lax.dynamic_index_in_dim(paired, head, 2, keepdims=False)
            live = (
                (doc_now[:, None] == key_doc[None, :])
                & (key_pos[None, :] <= pos_now[:, None])
                & (key_pos[None, :] >= 0)
            )

            def update(state, pair_head=pair_head, live=live):
                running, total, accum = state
                scores = (
                    jnp.einsum(
                        "rd,kd->rk", query_now, pair_head[0], preferred_element_type=jnp.float32
                    )
                    * scale
                )
                scores = jnp.where(live, scores, -1e30)
                newest = jnp.maximum(running, jnp.max(scores, axis=1))
                weights = jnp.where(live, jnp.exp(scores - newest[:, None]), 0.0)
                factor = jnp.exp(running - newest)
                total = total * factor + jnp.sum(weights, axis=1)
                accum = accum * factor[:, None] + jnp.dot(
                    weights.astype(jnp.bfloat16), pair_head[1], preferred_element_type=jnp.float32
                )
                return (newest, total, accum)

            carry = update(carry)
        return (carry[2] / carry[1][:, None]).astype(jnp.bfloat16)

    results = lax.map(one_item, jnp.arange(kv_local * parts, dtype=jnp.int32))
    results = results.reshape(kv_local, group, count, width_head)
    return jnp.transpose(results, (2, 0, 1, 3))


def per_device(queries, keys, values, lengths):
    groups = lax.axis_size("head")
    seq_index = lax.axis_index("seq")
    tok = queries.shape[0]
    shard = tok * groups
    ends = jnp.cumsum(lengths)
    q_split = queries.reshape(tok, groups, H // groups * DH)
    k_split = keys.reshape(tok, groups, KVH // groups * DH)
    v_split = values.reshape(tok, groups, KVH // groups * DH)
    q_here, k_here, v_here = (
        lax.all_to_all(q_split, "head", split_axis=1, concat_axis=0, tiled=True),
        lax.all_to_all(k_split, "head", split_axis=1, concat_axis=0, tiled=True),
        lax.all_to_all(v_split, "head", split_axis=1, concat_axis=0, tiled=True),
    )
    query_heads = q_here.reshape(shard, KVH // groups, H // KVH, DH)
    own = jnp.stack([k_here, v_here])
    earlier = earlier_blocks(own)
    query_pos = seq_index * shard + jnp.arange(shard, dtype=jnp.int32)
    blocks = [(own, query_pos)]
    for step in range(REACH):
        blocks.append((earlier[step], query_pos - (step + 1) * shard))
    mixed = attend(query_heads, query_pos, blocks, ends)
    mixed = mixed.reshape(shard, 1, H // groups * DH)
    returned = lax.all_to_all(mixed, "head", split_axis=0, concat_axis=1, tiled=True)
    return returned.reshape(tok, H * DH)


def solution(mesh):
    return jax.shard_map(
        per_device,
        mesh=mesh,
        in_specs=(
            P(("seq", "head"), None),
            P(("seq", "head"), None),
            P(("seq", "head"), None),
            P(),
        ),
        out_specs=P(("seq", "head"), None),
        check_vma=False,
    )
```

profile of v0, /device:TPU:33, one launch (start us, length us, event | category | flops | bytes accessed | tf_op | source)
XLA Modules:
  0.0 420.3 jit_solution(15559182435434750051)
XLA Ops:
  1.8 9.7 %all-to-all-start.2 = ((bf16[128,8,128]{0,2,1:T(8,128)(2,1)}), bf16[128,8,128]{0,2,1:T(8,128)(2,1)S(1)}, u32[]{:S(2)}, u32[]{:S(2)}) async-start(bf16[128,8,128]{0,2,1:T(8,128)(2,1)} %bitcast.9), calls=%async_computation.2 | async-start | bytes 524288 | tf_op jit(solution)/shard_map/all_to_all | solution.py:104
  13.3 10.7 %all-to-all-done.2 = bf16[128,8,128]{0,2,1:T(8,128)(2,1)S(1)} async-done(((bf16[128,8,128]{0,2,1:T(8,128)(2,1)}), bf16[128,8,128]{0,2,1:T(8,128)(2,1)S(1)}, u32[]{:S(2)}, u32[]{:S(2)}) %all-to-all-start.2) | async-done | bytes 262176 | tf_op jit(solution)/shard_map/all_to_all | solution.py:104
  24.0 3.4 all-to-all-start.1
  27.5 3.2 copy.52
  30.6 6.7 %all-to-all-done.1 = bf16[128,8,128]{0,2,1:T(8,128)(2,1)S(1)} async-done(((bf16[128,8,128]{0,2,1:T(8,128)(2,1)}), bf16[128,8,128]{0,2,1:T(8,128)(2,1)S(1)}, u32[]{:S(2)}, u32[]{:S(2)}) %all-to-all-start.1) | async-done | bytes 262176 | tf_op jit(solution)/shard_map/all_to_all | solution.py:103
  37.4 3.6 all-to-all-start
  41.4 6.6 %collective-permute-start = (bf16[2,1024,1,128]{3,1,2,0:T(8,128)(2,1)S(1)}, bf16[2,1024,1,128]{3,1,2,0:T(8,128)(2,1)}, u32[]{:S(2)}, u32[]{:S(2)}) collective-permute-start(bf16[2,1024,1,128]{3,1,2,0:T(8,128)(2,1)S(1)} %pad_maximum_fusion), channel_id=1, source_target_pairs={{0,8},{8,16},{16,24},{24,32},{32,40},{40,48},{48,56},{56,64},{64,7... | collective-permute-start | bytes 1572872 | tf_op jit(solution)/shard_map/ppermute | solution.py:17
  48.0 3.2 collective-permute-start.1
  51.8 38.4 %all-to-all-done = bf16[128,8,1024]{2,0,1:T(8,128)(2,1)S(1)} async-done(((bf16[128,8,1024]{2,0,1:T(8,128)(2,1)}), bf16[128,8,1024]{2,0,1:T(8,128)(2,1)S(1)}, u32[]{:S(2)}, u32[]{:S(2)}) %all-to-all-start) | async-done | bytes 2097184 | tf_op jit(solution)/shard_map/all_to_all | solution.py:102
  91.1 13.7 %collective-permute-done.1 = bf16[2,1024,1,128]{3,1,2,0:T(8,128)(2,1)} collective-permute-done((bf16[2,1024,1,128]{3,1,2,0:T(8,128)(2,1)S(1)}, bf16[2,1024,1,128]{3,1,2,0:T(8,128)(2,1)}, u32[]{:S(2)}, u32[]{:S(2)}) %collective-permute-start.1) | collective-permute-done | bytes 524320 | tf_op jit(solution)/shard_map/ppermute | solution.py:17
  104.8 228.3 %while.14 = (s32[]{:T(128)}, bf16[8,1024,128]{1,2,0:T(8,128)(2,1)}, s32[8]{0:T(128)S(1)}, s32[8,1024]{1,0:T(8,128)S(1)}, s32[1024]{0:T(1024)S(1)}, /*index=5*/s3...) while((s32[]{:T(128)}, bf16[8,1024,128]{1,2,0:T(8,128)(2,1)}, ...), condition=%wide.region_11.12_spmd.clone.clone, body=%wide.region_4.11_spmd.clone.clone.sunk | while | flops 1690193920 | bytes 52192112 | solution.py:87
  111.6 5.5 %fusion.120 = (f32[1024]{0:T(1024)S(1)}, f32[1024]{0:T(1024)S(1)}, f32[1024]{0:T(1024)S(1)}, f32[1024,1024]{0,1:T(8,128)S(1)}) fusion(pred[1024]{0:T(1024)(128)(4,1)S(1)} %get-tuple-element.462, s32[1024]{0:T(1024)S(1)} %bitcast.108, s32[1024]{0:T(1024)S(1)} %get-tuple-element.464, s32[1024]{0:T(1024)S(1)} %get-tuple-element.526, ...), kind=kOutput, calls=%fused_computation.14.clone.1 | convolution fusion | flops 290452480 | bytes 13155332 | tf_op jit(solution)/shard_map/while/body/eval_jaxpr/rd,kd->rk/dot_general | solution.py:69
  117.1 7.0 %fusion.122 = (f32[1024]{0:T(1024)S(1)}, f32[1024]{0:T(1024)S(1)}, f32[1024]{0:T(1024)S(1)}) fusion(f32[1024,1024]{0,1:T(8,128)S(1)} %fusion.116, f32[1024]{0:T(1024)S(1)} %get-tuple-element.471, pred[1024]{0:T(1024)(128)(4,1)S(1)} %get-tuple-element.466, s32[1024]{0:T(1024)S(1)} %bitcast.109, s32[1024]{0:T(1024)S(1)} %get-tuple-element.467, ...), kind=kLoop, calls=%fused_computation.15.clone.1 | loop fusion | flops 28308480 | bytes 12643328 | tf_op jit(solution)/shard_map/while/body/eval_jaxpr/reduce_sum | solution.py:78
  126.4 3.1 fusion.124
  129.6 3.1 fusion.125
  140.1 5.5 %fusion.120 = (f32[1024]{0:T(1024)S(1)}, f32[1024]{0:T(1024)S(1)}, f32[1024]{0:T(1024)S(1)}, f32[1024,1024]{0,1:T(8,128)S(1)}) fusion(pred[1024]{0:T(1024)(128)(4,1)S(1)} %get-tuple-element.462, s32[1024]{0:T(1024)S(1)} %bitcast.108, s32[1024]{0:T(1024)S(1)} %get-tuple-element.464, s32[1024]{0:T(1024)S(1)} %get-tuple-element.526, ...), kind=kOutput, calls=%fused_computation.14.clone.1 | convolution fusion | flops 290452480 | bytes 13155332 | tf_op jit(solution)/shard_map/while/body/eval_jaxpr/rd,kd->rk/dot_general | solution.py:69
  145.6 7.0 %fusion.122 = (f32[1024]{0:T(1024)S(1)}, f32[1024]{0:T(1024)S(1)}, f32[1024]{0:T(1024)S(1)}) fusion(f32[1024,1024]{0,1:T(8,128)S(1)} %fusion.116, f32[1024]{0:T(1024)S(1)} %get-tuple-element.471, pred[1024]{0:T(1024)(128)(4,1)S(1)} %get-tuple-element.466, s32[1024]{0:T(1024)S(1)} %bitcast.109, s32[1024]{0:T(1024)S(1)} %get-tuple-element.467, ...), kind=kLoop, calls=%fused_computation.15.clone.1 | loop fusion | flops 28308480 | bytes 12643328 | tf_op jit(solution)/shard_map/while/body/eval_jaxpr/reduce_sum | solution.py:78
  154.9 3.1 fusion.124
  158.1 3.1 fusion.125
  168.7 5.5 %fusion.120 = (f32[1024]{0:T(1024)S(1)}, f32[1024]{0:T(1024)S(1)}, f32[1024]{0:T(1024)S(1)}, f32[1024,1024]{0,1:T(8,128)S(1)}) fusion(pred[1024]{0:T(1024)(128)(4,1)S(1)} %get-tuple-element.462, s32[1024]{0:T(1024)S(1)} %bitcast.108, s32[1024]{0:T(1024)S(1)} %get-tuple-element.464, s32[1024]{0:T(1024)S(1)} %get-tuple-element.526, ...), kind=kOutput, calls=%fused_computation.14.clone.1 | convolution fusion | flops 290452480 | bytes 13155332 | tf_op jit(solution)/shard_map/while/body/eval_jaxpr/rd,kd->rk/dot_general | solution.py:69
  174.1 7.0 %fusion.122 = (f32[1024]{0:T(1024)S(1)}, f32[1024]{0:T(1024)S(1)}, f32[1024]{0:T(1024)S(1)}) fusion(f32[1024,1024]{0,1:T(8,128)S(1)} %fusion.116, f32[1024]{0:T(1024)S(1)} %get-tuple-element.471, pred[1024]{0:T(1024)(128)(4,1)S(1)} %get-tuple-element.466, s32[1024]{0:T(1024)S(1)} %bitcast.109, s32[1024]{0:T(1024)S(1)} %get-tuple-element.467, ...), kind=kLoop, calls=%fused_computation.15.clone.1 | loop fusion | flops 28308480 | bytes 12643328 | tf_op jit(solution)/shard_map/while/body/eval_jaxpr/reduce_sum | solution.py:78
  183.4 3.1 fusion.124
  186.6 3.1 fusion.125
  197.2 5.5 %fusion.120 = (f32[1024]{0:T(1024)S(1)}, f32[1024]{0:T(1024)S(1)}, f32[1024]{0:T(1024)S(1)}, f32[1024,1024]{0,1:T(8,128)S(1)}) fusion(pred[1024]{0:T(1024)(128)(4,1)S(1)} %get-tuple-element.462, s32[1024]{0:T(1024)S(1)} %bitcast.108, s32[1024]{0:T(1024)S(1)} %get-tuple-element.464, s32[1024]{0:T(1024)S(1)} %get-tuple-element.526, ...), kind=kOutput, calls=%fused_computation.14.clone.1 | convolution fusion | flops 290452480 | bytes 13155332 | tf_op jit(solution)/shard_map/while/body/eval_jaxpr/rd,kd->rk/dot_general | solution.py:69
  202.7 7.0 %fusion.122 = (f32[1024]{0:T(1024)S(1)}, f32[1024]{0:T(1024)S(1)}, f32[1024]{0:T(1024)S(1)}) fusion(f32[1024,1024]{0,1:T(8,128)S(1)} %fusion.116, f32[1024]{0:T(1024)S(1)} %get-tuple-element.471, pred[1024]{0:T(1024)(128)(4,1)S(1)} %get-tuple-element.466, s32[1024]{0:T(1024)S(1)} %bitcast.109, s32[1024]{0:T(1024)S(1)} %get-tuple-element.467, ...), kind=kLoop, calls=%fused_computation.15.clone.1 | loop fusion | flops 28308480 | bytes 12643328 | tf_op jit(solution)/shard_map/while/body/eval_jaxpr/reduce_sum | solution.py:78
  211.9 3.1 fusion.124
  215.1 3.1 fusion.125
  225.7 5.5 %fusion.120 = (f32[1024]{0:T(1024)S(1)}, f32[1024]{0:T(1024)S(1)}, f32[1024]{0:T(1024)S(1)}, f32[1024,1024]{0,1:T(8,128)S(1)}) fusion(pred[1024]{0:T(1024)(128)(4,1)S(1)} %get-tuple-element.462, s32[1024]{0:T(1024)S(1)} %bitcast.108, s32[1024]{0:T(1024)S(1)} %get-tuple-element.464, s32[1024]{0:T(1024)S(1)} %get-tuple-element.526, ...), kind=kOutput, calls=%fused_computation.14.clone.1 | convolution fusion | flops 290452480 | bytes 13155332 | tf_op jit(solution)/shard_map/while/body/eval_jaxpr/rd,kd->rk/dot_general | solution.py:69
  231.2 7.0 %fusion.122 = (f32[1024]{0:T(1024)S(1)}, f32[1024]{0:T(1024)S(1)}, f32[1024]{0:T(1024)S(1)}) fusion(f32[1024,1024]{0,1:T(8,128)S(1)} %fusion.116, f32[1024]{0:T(1024)S(1)} %get-tuple-element.471, pred[1024]{0:T(1024)(128)(4,1)S(1)} %get-tuple-element.466, s32[1024]{0:T(1024)S(1)} %bitcast.109, s32[1024]{0:T(1024)S(1)} %get-tuple-element.467, ...), kind=kLoop, calls=%fused_computation.15.clone.1 | loop fusion | flops 28308480 | bytes 12643328 | tf_op jit(solution)/shard_map/while/body/eval_jaxpr/reduce_sum | solution.py:78
  240.5 3.1 fusion.124
  243.6 3.1 fusion.125
  254.2 5.5 %fusion.120 = (f32[1024]{0:T(1024)S(1)}, f32[1024]{0:T(1024)S(1)}, f32[1024]{0:T(1024)S(1)}, f32[1024,1024]{0,1:T(8,128)S(1)}) fusion(pred[1024]{0:T(1024)(128)(4,1)S(1)} %get-tuple-element.462, s32[1024]{0:T(1024)S(1)} %bitcast.108, s32[1024]{0:T(1024)S(1)} %get-tuple-element.464, s32[1024]{0:T(1024)S(1)} %get-tuple-element.526, ...), kind=kOutput, calls=%fused_computation.14.clone.1 | convolution fusion | flops 290452480 | bytes 13155332 | tf_op jit(solution)/shard_map/while/body/eval_jaxpr/rd,kd->rk/dot_general | solution.py:69
  259.7 7.0 %fusion.122 = (f32[1024]{0:T(1024)S(1)}, f32[1024]{0:T(1024)S(1)}, f32[1024]{0:T(1024)S(1)}) fusion(f32[1024,1024]{0,1:T(8,128)S(1)} %fusion.116, f32[1024]{0:T(1024)S(1)} %get-tuple-element.471, pred[1024]{0:T(1024)(128)(4,1)S(1)} %get-tuple-element.466, s32[1024]{0:T(1024)S(1)} %bitcast.109, s32[1024]{0:T(1024)S(1)} %get-tuple-element.467, ...), kind=kLoop, calls=%fused_computation.15.clone.1 | loop fusion | flops 28308480 | bytes 12643328 | tf_op jit(solution)/shard_map/while/body/eval_jaxpr/reduce_sum | solution.py:78
  269.0 3.1 fusion.124
  272.1 3.1 fusion.125
  282.7 5.5 %fusion.120 = (f32[1024]{0:T(1024)S(1)}, f32[1024]{0:T(1024)S(1)}, f32[1024]{0:T(1024)S(1)}, f32[1024,1024]{0,1:T(8,128)S(1)}) fusion(pred[1024]{0:T(1024)(128)(4,1)S(1)} %get-tuple-element.462, s32[1024]{0:T(1024)S(1)} %bitcast.108, s32[1024]{0:T(1024)S(1)} %get-tuple-element.464, s32[1024]{0:T(1024)S(1)} %get-tuple-element.526, ...), kind=kOutput, calls=%fused_computation.14.clone.1 | convolution fusion | flops 290452480 | bytes 13155332 | tf_op jit(solution)/shard_map/while/body/eval_jaxpr/rd,kd->rk/dot_general | solution.py:69
  288.2 7.0 %fusion.122 = (f32[1024]{0:T(1024)S(1)}, f32[1024]{0:T(1024)S(1)}, f32[1024]{0:T(1024)S(1)}) fusion(f32[1024,1024]{0,1:T(8,128)S(1)} %fusion.116, f32[1024]{0:T(1024)S(1)} %get-tuple-element.471, pred[1024]{0:T(1024)(128)(4,1)S(1)} %get-tuple-element.466, s32[1024]{0:T(1024)S(1)} %bitcast.109, s32[1024]{0:T(1024)S(1)} %get-tuple-element.467, ...), kind=kLoop, calls=%fused_computation.15.clone.1 | loop fusion | flops 28308480 | bytes 12643328 | tf_op jit(solution)/shard_map/while/body/eval_jaxpr/reduce_sum | solution.py:78
  297.5 3.1 fusion.124
  300.6 3.1 fusion.125
  311.2 5.5 %fusion.120 = (f32[1024]{0:T(1024)S(1)}, f32[1024]{0:T(1024)S(1)}, f32[1024]{0:T(1024)S(1)}, f32[1024,1024]{0,1:T(8,128)S(1)}) fusion(pred[1024]{0:T(1024)(128)(4,1)S(1)} %get-tuple-element.462, s32[1024]{0:T(1024)S(1)} %bitcast.108, s32[1024]{0:T(1024)S(1)} %get-tuple-element.464, s32[1024]{0:T(1024)S(1)} %get-tuple-element.526, ...), kind=kOutput, calls=%fused_computation.14.clone.1 | convolution fusion | flops 290452480 | bytes 13155332 | tf_op jit(solution)/shard_map/while/body/eval_jaxpr/rd,kd->rk/dot_general | solution.py:69
  316.7 7.0 %fusion.122 = (f32[1024]{0:T(1024)S(1)}, f32[1024]{0:T(1024)S(1)}, f32[1024]{0:T(1024)S(1)}) fusion(f32[1024,1024]{0,1:T(8,128)S(1)} %fusion.116, f32[1024]{0:T(1024)S(1)} %get-tuple-element.471, pred[1024]{0:T(1024)(128)(4,1)S(1)} %get-tuple-element.466, s32[1024]{0:T(1024)S(1)} %bitcast.109, s32[1024]{0:T(1024)S(1)} %get-tuple-element.467, ...), kind=kLoop, calls=%fused_computation.15.clone.1 | loop fusion | flops 28308480 | bytes 12643328 | tf_op jit(solution)/shard_map/while/body/eval_jaxpr/reduce_sum | solution.py:78
  326.0 3.1 fusion.124
  329.2 3.1 fusion.125
  333.7 4.0 reduce.1
  340.3 6.3 %reshape.184 = bf16[8,2,65536]{2,1,0:T(2,128)(2,1)} reshape(bf16[1024,1024]{1,0:T(8,128)(2,1)} %copy.53) | data formatting | bytes 4194304
  346.5 59.9 %all_to_all.60 = bf16[8,2,65536]{2,1,0:T(2,128)(2,1)S(1)} all-to-all(bf16[8,2,65536]{2,1,0:T(2,128)(2,1)} %reshape.184), channel_id=1, replica_groups=mesh['seq'=32,'head'=8] {'head'}, dimensions={0} | all-to-all | bytes 4194304 | tf_op jit(solution)/shard_map/all_to_all | solution.py:115
  406.5 4.4 %reshape.185 = bf16[1024,1,1024]{2,1,0:T(2,128)(2,1)} reshape(bf16[8,2,65536]{2,1,0:T(2,128)(2,1)S(1)} %all_to_all.60) | data formatting | bytes 4194304
  416.3 4.1 copy.45
  (128 shorter events, 64.0 us)
Async XLA Ops:
  1.8 22.2 %all-to-all-start.2 = ((bf16[128,8,128]{0,2,1:T(8,128)(2,1)}), bf16[128,8,128]{0,2,1:T(8,128)(2,1)S(1)}, u32[]{:S(2)}, u32[]{:S(2)}) async-start(bf16[128,8,128]{0,2,1:T(8,128)(2,1)} %bitcast.9), calls=%async_computation.2 | async-start | bytes 524288 | tf_op jit(solution)/shard_map/all_to_all | solution.py:104
  24.0 13.3 %all-to-all-start.1 = ((bf16[128,8,128]{0,2,1:T(8,128)(2,1)}), bf16[128,8,128]{0,2,1:T(8,128)(2,1)S(1)}, u32[]{:S(2)}, u32[]{:S(2)}) async-start(bf16[128,8,128]{0,2,1:T(8,128)(2,1)} %bitcast.5), calls=%async_computation.1 | async-start | bytes 524288 | tf_op jit(solution)/shard_map/all_to_all | solution.py:103
  30.6 20.6 %copy-start = (s32[64]{0:T(128)S(1)}, s32[64]{0:T(128)}, u32[]{:S(2)}) copy-start(s32[64]{0:T(128)} %param.9) | copy-start | bytes 772
  37.4 52.8 %all-to-all-start = ((bf16[128,8,1024]{2,0,1:T(8,128)(2,1)}), bf16[128,8,1024]{2,0,1:T(8,128)(2,1)S(1)}, u32[]{:S(2)}, u32[]{:S(2)}) async-start(bf16[128,8,1024]{2,0,1:T(8,128)(2,1)} %bitcast.71), calls=%async_computation | async-start | bytes 4194304 | tf_op jit(solution)/shard_map/all_to_all | solution.py:102
  41.4 49.7 %collective-permute-start = (bf16[2,1024,1,128]{3,1,2,0:T(8,128)(2,1)S(1)}, bf16[2,1024,1,128]{3,1,2,0:T(8,128)(2,1)}, u32[]{:S(2)}, u32[]{:S(2)}) collective-permute-start(bf16[2,1024,1,128]{3,1,2,0:T(8,128)(2,1)S(1)} %pad_maximum_fusion), channel_id=1, source_target_pairs={{0,8},{8,16},{16,24},{24,32},{32,40},{40,48},{48,56},{56,64},{64,7... | collective-permute-start | bytes 1572872 | tf_op jit(solution)/shard_map/ppermute | solution.py:17
  48.0 56.8 %collective-permute-start.1 = (bf16[2,1024,1,128]{3,1,2,0:T(8,128)(2,1)S(1)}, bf16[2,1024,1,128]{3,1,2,0:T(8,128)(2,1)}, u32[]{:S(2)}, u32[]{:S(2)}) collective-permute-start(bf16[2,1024,1,128]{3,1,2,0:T(8,128)(2,1)S(1)} %pad_maximum_fusion), channel_id=1, source_target_pairs={{0,16},{8,24},{16,32},{24,40},{32,48},{40,56},{48,64},{56,72},{64,... | collective-permute-start | bytes 1572872 | tf_op jit(solution)/shard_map/ppermute | solution.py:17
where the time goes:
time: 422 us; the launch traced here: 420 us
  matrix products  131 us (31%)
  waiting for transfers between devices  69.5 us (16%)
  other arithmetic  60.5 us (14%)
  blocking collectives  59.9 us (14%)
  local copies, waits for them, and re-layouts  43.8 us (10%)
  loops' own time  28.7 us (7%)
  starting transfers between devices  26.6 us (6%)
    dot_general x24, matrix products, update(): jnp.dot(weights.astype(jnp.bfloat16), pair_head[1], preferred_element_typ...  68.4 us
    dot_general x24, matrix products, update(): jnp.einsum('rd,kd->rk', query_now, pair_head[0], preferred_element_type=j...  62.7 us
    all_to_all x1, blocking collectives, per_device(): lax.all_to_all(mixed, 'head', split_axis=0, concat_axis=1, tiled=True)  59.9 us
    reduce_sum x8, other arithmetic, update(): total = total * factor + jnp.sum(weights, axis=1)  55.7 us
    all_to_all x1, waiting for transfers between devices, per_device(): lax.all_to_all(q_split, 'head', split_axis=1, concat_axis=0, tiled=True)  38.4 us
    another operation x1, loops' own time, attend(): results = lax.map(one_item, jnp.arange(kv_local * parts, dtype=jnp.int32))  28.7 us
    unnamed x10, local copies, waits for them, and re-layouts  20.7 us
    ppermute x2, waiting for transfers between devices, shifted(): lax.ppermute(value, axis, [(source, source + steps) for source in range(l...  13.7 us
  transfers between devices with their start and end apart: 5, of which 4 were waited for; matrix products, arithmetic and copies ran while one was open for 2% of the time, Pallas kernels for 0%

commit v1 on v0

v1 whole, which is shorter than its diff:
```python
import functools
import math

import jax
import jax.numpy as jnp
from jax import lax
from jax.experimental import pallas as pl
from jax.experimental.pallas import tpu as pltpu
from jax.sharding import PartitionSpec as P

H, KVH, DH = 64, 8, 128
GROUP = H // KVH
TOK = 128
ROWS = GROUP * TOK
BIG = 1e30
RATE = math.log2(math.e) / math.sqrt(DH)
MESH = pl.DeviceIdType.MESH


class Place:
    def __init__(self):
        self.s, self.h = s, h = lax.axis_index("seq"), lax.axis_index("head")
        self.core = lax.rem(s, 2)
        self.x, self.z = lax.rem(h, 4), h // 4
        self.own, self.other = self.z * 4, 4 - self.z * 4
        self.xl, self.xr, self.xo = (lax.rem(self.x + d, 4) for d in (3, 1, 2))
        self.right, self.left = (s, self.own + self.xr), (s, self.own + self.xl)
        self.far = (s, self.other + self.x)
        self.twin = (s + 1 - 2 * self.core, h)
        self.later, self.before = (s + 2, h), (s - 2, h)
        self.has_later, self.has_before = s < 30, s >= 2


def when(cond, action):
    if cond is None:
        action()
    else:
        pl.when(cond)(action)


def spread(column, width):
    return jnp.concatenate([column] * (width // 128), axis=1)


def kernel(
    q_hbm, k_hbm, v_hbm, len_ref, o_hbm,
    kv, q_raw, qa, km, acc, top, tot, out, bounds,
    load_sem, out_sem, ss_x, ss_c, ss_y, ss_z, rs,
):
    p = Place()
    s, h, core, x = p.s, p.h, p.core, p.x
    loads = [
        pltpu.make_async_copy(k_hbm, kv.at[0, h, 0], load_sem.at[0]),
        pltpu.make_async_copy(v_hbm, kv.at[0, h, 1], load_sem.at[1]),
        pltpu.make_async_copy(q_hbm, q_raw, load_sem.at[2]),
    ]
    for load in loads:
        load.start()

    barrier = pltpu.get_barrier_semaphore()

    def greet(device):
        pl.semaphore_signal(barrier, inc=1, device_id=device, device_id_type=MESH)

    for device in (p.left, p.right, p.far, p.twin):
        greet(device)
    when(p.has_before, lambda: greet(p.before))
    when(p.has_later, lambda: greet(p.later))

    @pl.when(s < 2)
    def _():
        kv[2] = jnp.zeros(kv.shape[1:], kv.dtype)

    @pl.when(s == 0)
    def _():
        kv[1] = jnp.zeros(kv.shape[1:], kv.dtype)

    pl.semaphore_wait(barrier, 4 + p.has_before.astype(jnp.int32) + p.has_later.astype(jnp.int32))
    loads[0].wait()
    loads[1].wait()

    sends = []

    def send(cond, src, dst, sem, device):
        copy = pltpu.make_async_remote_copy(
            src_ref=kv.at[src], dst_ref=kv.at[dst], send_sem=sem, recv_sem=rs.at[dst],
            device_id=device, device_id_type=MESH,
        )
        when(cond, copy.start)
        sends.append((cond, copy))

    def arrived(cond, where):
        copy = pltpu.make_async_remote_copy(
            src_ref=kv.at[where], dst_ref=kv.at[where], send_sem=ss_z.at[0], recv_sem=rs.at[where],
            device_id=p.right, device_id_type=MESH,
        )
        when(cond, copy.wait_recv)

    def modes(row, other):
        gathers = core == row // 2
        on = (s >= 2) if row == 2 else (s >= 0)
        if other:
            return on & (gathers | (core == p.z)), None, on & gathers
        return on & gathers, on & jnp.logical_not(gathers), on & gathers

    def begin(phase, row, other):
        full, part, gathers = modes(row, other)
        slot = (p.other if other else p.own) + x
        to_right, to_left = full, full
        if part is not None:
            if row == 0:
                to_right, to_left = full | part & (x < 3), full | part & (x == 0)
            else:
                to_right, to_left = full | part & (x == 3), full | part & (x > 0)
        for t in range(2):
            here = (row, slot, t)
            send(to_right, here, here, ss_x.at[phase, t], p.right)
            send(to_left, here, here, ss_x.at[phase, 2 + t], p.left)
            send(gathers, here, (1, slot, t), ss_c.at[slot, t], p.twin)

    def middle(phase, row, other):
        full, part, gathers = modes(row, other)
        base = p.other if other else p.own
        sl, sr = base + p.xl, base + p.xr
        inner = (x == 1) | (x == 2)
        from_left, from_right = full, full
        on_right, on_left = [full, None], [None, full]
        if part is not None:
            if row == 0:
                from_left, from_right = full | part & (x > 0), full | part & (x == 3)
                on_right = [full | part & inner, part & inner]
            else:
                from_left, from_right = full | part & (x == 0), full | part & (x < 3)
                on_left = [part & inner, full | part & inner]
        for t in range(2):
            here = (row, sl, t)
            arrived(from_left, here)
            if on_right[t] is not None:
                send(on_right[t], here, here, ss_x.at[phase, 4 + t], p.right)
            send(gathers, here, (1, sl, t), ss_c.at[sl, t], p.twin)
            here = (row, sr, t)
            arrived(from_right, here)
            if on_left[t] is not None:
                send(on_left[t], here, here, ss_x.at[phase, 6 + t], p.left)
            send(gathers, here, (1, sr, t), ss_c.at[sr, t], p.twin)

    def end(phase, row, other):
        full, part, gathers = modes(row, other)
        so = (p.other if other else p.own) + p.xo
        got = full
        if part is not None:
            got = full | part & ((x >= 2) if row == 0 else (x < 2))
        for t in range(2):
            here = (row, so, t)
            arrived(got, here)
            send(gathers, here, (1, so, t), ss_c.at[so, t], p.twin)

    def twin_sent(slots):
        for slot in slots:
            for t in range(2):
                arrived(s >= 1, (1, slot, t))

    def block_mask(row, slot):
        pos = ((s - row) * 8 + slot) * TOK + lax.broadcasted_iota(jnp.int32, (TOK, DH), 0)
        starts, ends = bounds[0:1, :], bounds[1:2, :]
        return jnp.where((pos >= starts) & (pos < ends), 0.0, -BIG).astype(jnp.bfloat16)

    def attend(blocks, first=False, last=False):
        count = len(blocks)
        width = count * TOK
        for i, (row, slot) in enumerate(blocks):
            km[i * TOK:(i + 1) * TOK, :] = block_mask(row, slot)

        def one_head(j, carry):
            lanes = pl.ds(pl.multiple_of(j * DH, DH), DH)
            keys = jnp.concatenate([kv[row, slot, 0, :, lanes] for row, slot in blocks], axis=0)
            keys = jnp.concatenate([keys, km[0:width, :]], axis=1)
            values = jnp.concatenate([kv[row, slot, 1, :, lanes] for row, slot in blocks], axis=0)
            values = jnp.concatenate([values, jnp.ones((width, DH), jnp.bfloat16)], axis=1)
            for part in range(ROWS // CHUNK):
                rows = pl.ds(part * CHUNK, CHUNK)
                scores = lax.dot_general(
                    qa[j, rows, :], keys, (((1,), (1,)), ((), ())), preferred_element_type=jnp.float32
                )
                if first:
                    token = lax.broadcasted_iota(jnp.int32, (CHUNK, width), 0) & (TOK - 1)
                    key = lax.broadcasted_iota(jnp.int32, (CHUNK, width), 1)
                    scores = jnp.where(key <= token, scores, -BIG)
                best = jnp.broadcast_to(jnp.max(scores, axis=1, keepdims=True), (CHUNK, DH))
                if not first:
                    old = top[j, rows, :]
                    best = jnp.maximum(best, old)
                weights = jnp.exp2((scores - spread(best, width)) * RATE).astype(jnp.bfloat16)
                both = jnp.dot(weights, values, preferred_element_type=jnp.float32)
                mixed, total = both[:, :DH], both[:, DH:]
                if not first:
                    factor = jnp.exp2((old - best) * RATE)
                    mixed = mixed + acc[j, rows, :] * factor
                    total = total + tot[j, rows, :] * factor
                if last:
                    done = (mixed / total).astype(jnp.bfloat16)
                    for g in range(CHUNK // TOK):
                        column = (j * GROUP + part * (CHUNK // TOK) + g) * DH
                        out[:, pl.ds(pl.multiple_of(column, DH), DH)] = done[g * TOK:(g + 1) * TOK]
                else:
                    top[j, rows, :] = best
                    acc[j, rows, :] = mixed
                    tot[j, rows, :] = total
            if last:
                columns = pl.ds(pl.multiple_of(j * GROUP * DH, DH), GROUP * DH)
                pltpu.make_async_copy(out.at[:, columns], o_hbm.at[:, columns], out_sem.at[j]).start()
            return carry

        lax.fori_loop(0, KVH, one_head, 0)

    far = p.other + x
    wanted = (core == 1) | (p.z == 0)
    for t in range(2):
        send(p.has_later, (0, h, t), (2, h, t), ss_y.at[0, t], p.later)
    for t in range(2):
        send(None, (0, h, t), (0, h, t), ss_z.at[t], p.far)
    begin(0, 0, False)

    lens = jnp.concatenate([len_ref[...], jnp.zeros((1, DH - len_ref.shape[1]), jnp.int32)], axis=1)
    lens = jnp.broadcast_to(lens, (8, DH))
    lane = lax.broadcasted_iota(jnp.int32, (8, DH), 1)
    ends = lens
    for step in (1, 2, 4, 8, 16, 32, 64):
        ends = ends + jnp.where(lane >= step, pltpu.roll(ends, step, 1), 0)
    bounds[0:1, :] = (ends - lens)[0:1]
    bounds[1:2, :] = ends[0:1]
    pos = (s * 8 + h) * TOK + lax.broadcasted_iota(jnp.int32, (TOK, DH), 0)
    member = jnp.where((pos >= bounds[0:1, :]) & (pos < bounds[1:2, :]), 1.0, 0.0).astype(jnp.bfloat16)
    loads[2].wait()

    def arrange(j, carry):
        for g in range(GROUP):
            column = pl.multiple_of((j * GROUP + g) * DH, DH)
            qa[j, g * TOK:(g + 1) * TOK, 0:DH] = q_raw[:, pl.ds(column, DH)]
            qa[j, g * TOK:(g + 1) * TOK, DH:2 * DH] = member
        return carry

    lax.fori_loop(0, KVH, arrange, 0)

    attend([(0, h)], first=True)
    middle(0, 0, False)
    for t in range(2):
        arrived(p.has_before, (2, h, t))
    begin(1, 2, False)
    end(0, 0, False)
    middle(1, 2, False)
    for t in range(2):
        arrived(None, (0, far, t))
    for t in range(2):
        send(p.has_later & wanted, (0, far, t), (2, far, t), ss_y.at[1, t], p.later)
    begin(2, 0, True)
    end(1, 2, False)

    def mixed_row(other_x):
        return jnp.where(other_x < x, 0, 2)

    own, other = p.own, p.other
    attend([(mixed_row(d), own + d) for d in (p.xl, p.xr, p.xo)] + [(2, h)])
    middle(2, 0, True)
    twin_sent([own + d for d in range(4)])
    attend([(1, own + d) for d in range(4)])
    end(2, 0, True)
    for t in range(2):
        arrived(p.has_before & wanted, (2, far, t))
    begin(3, 2, True)

    late_both = (core == 0) & (p.z == 0)
    row_b = jnp.where(p.z == 0, 2, 0)
    first_row = jnp.where((core == 0) & (p.z == 1), row_b, 1)
    second_row = jnp.where((core == 0) & (p.z == 1), 1, row_b)
    order = [x, p.xl, p.xr, p.xo]
    plain = [(first_row, d) for d in order] + [(second_row, d) for d in order]
    paired = [(row, d) for d in order for row in (first_row, second_row)]
    todo = [
        (jnp.where(late_both, a, c), other + jnp.where(late_both, b, d))
        for (a, b), (c, d) in zip(paired, plain)
    ]


    for t in range(2):
        arrived(s >= 1, (1, far, t))
    early = (core == 1) & (s >= 1)
    for d in order[1:]:
        for t in range(2):
            arrived(early, (1, other + d, t))
    attend(todo[0:2])
    middle(3, 2, True)
    late = (core == 0) & (s >= 1)
    for d in order[1:3]:
        for t in range(2):
            arrived(late, (1, other + d, t))
    attend(todo[2:4])
    attend(todo[4:6])
    end(3, 2, True)
    for t in range(2):
        arrived(late, (1, other + p.xo, t))
    attend(todo[6:8], last=True)

    for cond, copy in sends:
        when(cond, copy.wait_send)
    for j in range(KVH):
        columns = pl.ds(j * GROUP * DH, GROUP * DH)
        pltpu.make_async_copy(out.at[:, columns], o_hbm.at[:, columns], out_sem.at[j]).wait()


CHUNK = 256


def per_device(queries, keys, values, lengths):
    tok = queries.shape[0]
    f32, bf16, dma = jnp.float32, jnp.bfloat16, pltpu.SemaphoreType.DMA
    return pl.pallas_call(
        kernel,
        out_shape=jax.ShapeDtypeStruct(queries.shape, bf16),
        in_specs=[pl.BlockSpec(memory_space=pl.ANY)] * 3 + [pl.BlockSpec(memory_space=pltpu.VMEM)],
        out_specs=pl.BlockSpec(memory_space=pl.ANY),
        scratch_shapes=[
            pltpu.VMEM((3, 8, 2, tok, KVH * DH), bf16),
            pltpu.VMEM((tok, H * DH), bf16),
            pltpu.VMEM((KVH, ROWS, 2 * DH), bf16),
            pltpu.VMEM((4 * tok, DH), bf16),
            pltpu.VMEM((KVH, ROWS, DH), f32),
            pltpu.VMEM((KVH, ROWS, DH), f32),
            pltpu.VMEM((KVH, ROWS, DH), f32),
            pltpu.VMEM((tok, H * DH), bf16),
            pltpu.VMEM((8, DH), jnp.int32),
            dma((3,)), dma((KVH,)), dma((4, 8)), dma((8, 2)), dma((2, 2)), dma((2,)), dma((3, 8, 2)),
        ],
        compiler_params=pltpu.CompilerParams(
            collective_id=0, has_side_effects=True, vmem_limit_bytes=56 << 20
        ),
        name="attend",
    )(queries, keys, values, lengths.reshape(1, -1))


def solution(mesh):
    spec = P(("seq", "head"), None)
    return jax.shard_map(
        per_device, mesh=mesh, in_specs=(spec, spec, spec, P()), out_specs=spec, check_vma=False
    )
```

time: 422 us -> 102 us (0.24)
  the two profiles are of different devices: /device:TPU:33 before, /device:TPU:216 now
where the time goes in v1:
time: 102 us
  Pallas kernels  98.8 us (97%)
  local copies, waits for them, and re-layouts  3.1 us (3%)
    pallas_call x1, Pallas kernels, per_device(): pl.pallas_call(kernel, out_shape=jax.ShapeDtypeStruct(queries.shape, bf16...  98.8 us
    unnamed x1, local copies, waits for them, and re-layouts  3.1 us

profile of v1, /device:TPU:216, one launch (start us, length us, event | category | flops | bytes accessed | tf_op | source)
XLA Modules:
  0.0 101.9 jit_solution(1545432704562168180)
XLA Ops:
  0.0 98.8 %attend.1 = bf16[128,8192]{1,0:T(8,128)(2,1)} custom-call(bf16[128,8192]{1,0:T(8,128)(2,1)} %q_hbm.1, bf16[128,1024]{1,0:T(8,128)(2,1)} %k_hbm.1, bf16[128,1024]{1,0:T(8,128)(2,1)} %v_hbm.1, s32[1,64]{1,0:T(1,128)} %bitcast.1), custom_call_target="tpu_custom_call" | custom-call | tf_op jit(solution)/shard_map/attend/pallas_call | solution.py:317
  98.8 3.1 %copy.6 = bf16[128,8192]{1,0:T(8,128)(2,1)} copy(bf16[128,8192]{1,0:T(8,128)(2,1)} %attend.1) | data formatting | bytes 4194304

commit v2 on v1

--- a/solution.py
+++ b/solution.py
@@ -21,7 +21,7 @@
     def __init__(self):
         self.s, self.h = s, h = lax.axis_index("seq"), lax.axis_index("head")
         self.core = lax.rem(s, 2)
-        self.x, self.z = lax.rem(h, 4), h // 4
+        self.x, self.y, self.z = lax.rem(h, 4), lax.rem(s // 2, 4), h // 4
         self.own, self.other = self.z * 4, 4 - self.z * 4
         self.xl, self.xr, self.xo = (lax.rem(self.x + d, 4) for d in (3, 1, 2))
         self.right, self.left = (s, self.own + self.xr), (s, self.own + self.xl)
@@ -76,18 +76,16 @@
         kv[1] = jnp.zeros(kv.shape[1:], kv.dtype)
 
     pl.semaphore_wait(barrier, 4 + p.has_before.astype(jnp.int32) + p.has_later.astype(jnp.int32))
-    loads[0].wait()
-    loads[1].wait()
-
     sends = []
 
-    def send(cond, src, dst, sem, device):
+    def send(cond, src, dst, sem, device, now=None):
         copy = pltpu.make_async_remote_copy(
-            src_ref=kv.at[src], dst_ref=kv.at[dst], send_sem=sem, recv_sem=rs.at[dst],
+            src_ref=src if not isinstance(src, tuple) else kv.at[src], dst_ref=kv.at[dst], send_sem=sem, recv_sem=rs.at[dst],
             device_id=device, device_id_type=MESH,
         )
-        when(cond, copy.start)
+        when(cond if now is None else now, copy.start)
         sends.append((cond, copy))
+        return copy
 
     def arrived(cond, where):
         copy = pltpu.make_async_remote_copy(
@@ -103,7 +101,7 @@
             return on & (gathers | (core == p.z)), None, on & gathers
         return on & gathers, on & jnp.logical_not(gathers), on & gathers
 
-    def begin(phase, row, other):
+    def begin(phase, row, other, t, source=None):
         full, part, gathers = modes(row, other)
         slot = (p.other if other else p.own) + x
         to_right, to_left = full, full
@@ -112,11 +110,11 @@
                 to_right, to_left = full | part & (x < 3), full | part & (x == 0)
             else:
                 to_right, to_left = full | part & (x == 3), full | part & (x > 0)
-        for t in range(2):
-            here = (row, slot, t)
-            send(to_right, here, here, ss_x.at[phase, t], p.right)
-            send(to_left, here, here, ss_x.at[phase, 2 + t], p.left)
-            send(gathers, here, (1, slot, t), ss_c.at[slot, t], p.twin)
+        here = (row, slot, t)
+        source = here if source is None else source
+        send(to_right, source, here, ss_x.at[phase, t], p.right)
+        send(to_left, source, here, ss_x.at[phase, 2 + t], p.left)
+        send(gathers, source, (1, slot, t), ss_c.at[slot, t], p.twin)
 
     def middle(phase, row, other):
         full, part, gathers = modes(row, other)
@@ -165,61 +163,70 @@
         starts, ends = bounds[0:1, :], bounds[1:2, :]
         return jnp.where((pos >= starts) & (pos < ends), 0.0, -BIG).astype(jnp.bfloat16)
 
-    def attend(blocks, first=False, last=False):
-        count = len(blocks)
-        width = count * TOK
+    def masks(blocks):
         for i, (row, slot) in enumerate(blocks):
             km[i * TOK:(i + 1) * TOK, :] = block_mask(row, slot)
 
-        def one_head(j, carry):
-            lanes = pl.ds(pl.multiple_of(j * DH, DH), DH)
-            keys = jnp.concatenate([kv[row, slot, 0, :, lanes] for row, slot in blocks], axis=0)
-            keys = jnp.concatenate([keys, km[0:width, :]], axis=1)
-            values = jnp.concatenate([kv[row, slot, 1, :, lanes] for row, slot in blocks], axis=0)
-            values = jnp.concatenate([values, jnp.ones((width, DH), jnp.bfloat16)], axis=1)
-            for part in range(ROWS // CHUNK):
-                rows = pl.ds(part * CHUNK, CHUNK)
-                scores = lax.dot_general(
-                    qa[j, rows, :], keys, (((1,), (1,)), ((), ())), preferred_element_type=jnp.float32
-                )
-                if first:
-                    token = lax.broadcasted_iota(jnp.int32, (CHUNK, width), 0) & (TOK - 1)
-                    key = lax.broadcasted_iota(jnp.int32, (CHUNK, width), 1)
-                    scores = jnp.where(key <= token, scores, -BIG)
-                best = jnp.broadcast_to(jnp.max(scores, axis=1, keepdims=True), (CHUNK, DH))
-                if not first:
-                    old = top[j, rows, :]
-                    best = jnp.maximum(best, old)
-                weights = jnp.exp2((scores - spread(best, width)) * RATE).astype(jnp.bfloat16)
-                both = jnp.dot(weights, values, preferred_element_type=jnp.float32)
-                mixed, total = both[:, :DH], both[:, DH:]
-                if not first:
-                    factor = jnp.exp2((old - best) * RATE)
-                    mixed = mixed + acc[j, rows, :] * factor
-                    total = total + tot[j, rows, :] * factor
-                if last:
-                    done = (mixed / total).astype(jnp.bfloat16)
-                    for g in range(CHUNK // TOK):
-                        column = (j * GROUP + part * (CHUNK // TOK) + g) * DH
-                        out[:, pl.ds(pl.multiple_of(column, DH), DH)] = done[g * TOK:(g + 1) * TOK]
-                else:
-                    top[j, rows, :] = best
-                    acc[j, rows, :] = mixed
-                    tot[j, rows, :] = total
+    def one_head(j, blocks, first, last):
+        width = len(blocks) * TOK
+        lanes = pl.ds(pl.multiple_of(j * DH, DH), DH)
+        keys = jnp.concatenate([kv[row, slot, 0, :, lanes] for row, slot in blocks], axis=0)
+        keys = jnp.concatenate([keys, km[0:width, :]], axis=1)
+        values = jnp.concatenate([kv[row, slot, 1, :, lanes] for row, slot in blocks], axis=0)
+        values = jnp.concatenate([values, jnp.ones((width, DH), jnp.bfloat16)], axis=1)
+        for part in range(ROWS // CHUNK):
+            rows = pl.ds(part * CHUNK, CHUNK)
+            scores = lax.dot_general(
+                qa[j, rows, :], keys, (((1,), (1,)), ((), ())), preferred_element_type=jnp.float32
+            )
+            if first:
+                token = lax.broadcasted_iota(jnp.int32, (CHUNK, width), 0) & (TOK - 1)
+                key = lax.broadcasted_iota(jnp.int32, (CHUNK, width), 1)
+                scores = jnp.where(key <= token, scores, -BIG)
+            best = jnp.broadcast_to(jnp.max(scores, axis=1, keepdims=True), (CHUNK, DH))
+            if not first:
+                old = top[j, rows, :]
+                best = jnp.maximum(best, old)
+            weights = jnp.exp2((scores - spread(best, width)) * RATE).astype(jnp.bfloat16)
+            both = jnp.dot(weights, values, preferred_element_type=jnp.float32)
+            mixed, total = both[:, :DH], both[:, DH:]
+            if not first:
+                factor = jnp.exp2((old - best) * RATE)
+                mixed = mixed + acc[j, rows, :] * factor
+                total = total + tot[j, rows, :] * factor
             if last:
-                columns = pl.ds(pl.multiple_of(j * GROUP * DH, DH), GROUP * DH)
-                pltpu.make_async_copy(out.at[:, columns], o_hbm.at[:, columns], out_sem.at[j]).start()
+                done = (mixed / total).astype(jnp.bfloat16)
+                for g in range(CHUNK // TOK):
+                    column = (j * GROUP + part * (CHUNK // TOK) + g) * DH
+                    out[:, pl.ds(pl.multiple_of(column, DH), DH)] = done[g * TOK:(g + 1) * TOK]
+            else:
+                top[j, rows, :] = best
+                acc[j, rows, :] = mixed
+                tot[j, rows, :] = total
+        if last:
+            columns = pl.ds(pl.multiple_of(j * GROUP * DH, DH), GROUP * DH)
+            pltpu.make_async_copy(out.at[:, columns], o_hbm.at[:, columns], out_sem.at[j]).start()
+
+    def attend(blocks, lo=0, hi=KVH, first=False, last=False):
+        if lo == 0:
+            masks(blocks)
+
+        def some_heads(turn, carry):
+            for j in range(UNROLL):
+                one_head(lo + turn * UNROLL + j, blocks, first, last)
             return carry
 
-        lax.fori_loop(0, KVH, one_head, 0)
+        lax.fori_loop(0, (hi - lo) // UNROLL, some_heads, 0)
 
     far = p.other + x
     wanted = (core == 1) | (p.z == 0)
-    for t in range(2):
-        send(p.has_later, (0, h, t), (2, h, t), ss_y.at[0, t], p.later)
-    for t in range(2):
-        send(None, (0, h, t), (0, h, t), ss_z.at[t], p.far)
-    begin(0, 0, False)
+    mine = (k_hbm, v_hbm)
+    for t in range(2):
+        send(p.has_later, mine[t], (2, h, t), ss_y.at[0, t], p.later)
+        begin(0, 0, False, t, mine[t])
+    crosses = p.y == 3
+    exchange = [send(None, mine[t], (0, h, t), ss_z.at[t], p.far, p.y != 3) for t in range(2)]
+
 
     lens = jnp.concatenate([len_ref[...], jnp.zeros((1, DH - len_ref.shape[1]), jnp.int32)], axis=1)
     lens = jnp.broadcast_to(lens, (8, DH))
@@ -242,32 +249,45 @@
 
     lax.fori_loop(0, KVH, arrange, 0)
 
+    loads[0].wait()
+    loads[1].wait()
     attend([(0, h)], first=True)
+
+    @pl.when(crosses)
+    def _():
+        for t in range(2):
+            when(p.has_later, sends[SHIFT[t]][1].wait_send)
+        for copy in exchange:
+            copy.start()
+
     middle(0, 0, False)
     for t in range(2):
         arrived(p.has_before, (2, h, t))
-    begin(1, 2, False)
+        begin(1, 2, False, t)
     end(0, 0, False)
     middle(1, 2, False)
     for t in range(2):
         arrived(None, (0, far, t))
-    for t in range(2):
         send(p.has_later & wanted, (0, far, t), (2, far, t), ss_y.at[1, t], p.later)
-    begin(2, 0, True)
+        begin(2, 0, True, t)
     end(1, 2, False)
 
     def mixed_row(other_x):
         return jnp.where(other_x < x, 0, 2)
 
     own, other = p.own, p.other
-    attend([(mixed_row(d), own + d) for d in (p.xl, p.xr, p.xo)] + [(2, h)])
+    mixed = [(mixed_row(d), own + d) for d in (p.xl, p.xr, p.xo)] + [(2, h)]
+    before = [(1, own + d) for d in range(4)]
+    attend(mixed, 0, 4)
+    attend(mixed, 4, 8)
     middle(2, 0, True)
+    for t in range(2):
+        arrived(p.has_before & wanted, (2, far, t))
+        begin(3, 2, True, t)
     twin_sent([own + d for d in range(4)])
-    attend([(1, own + d) for d in range(4)])
+    attend(before, 0, 4)
     end(2, 0, True)
-    for t in range(2):
-        arrived(p.has_before & wanted, (2, far, t))
-    begin(3, 2, True)
+    attend(before, 4, 8)
 
     late_both = (core == 0) & (p.z == 0)
     row_b = jnp.where(p.z == 0, 2, 0)
@@ -301,7 +321,9 @@
         arrived(late, (1, other + p.xo, t))
     attend(todo[6:8], last=True)
 
-    for cond, copy in sends:
+    for i, (cond, copy) in enumerate(sends):
+        if i in SHIFT:
+            cond = cond & jnp.logical_not(crosses)
         when(cond, copy.wait_send)
     for j in range(KVH):
         columns = pl.ds(j * GROUP * DH, GROUP * DH)
@@ -309,6 +331,8 @@
 
 
 CHUNK = 256
+UNROLL = 4
+SHIFT = (0, 4)
 
 
 def per_device(queries, keys, values, lengths):

time: 102 us -> 86.8 us (0.85)
  Pallas kernels: 98.8 us -> 83.3 us
    pallas_call x1, Pallas kernels: 98.8 us -> 83.3 us  [per_device(): pl.pallas_call(kernel, out_shape=jax.ShapeDtypeStruct(queries.shape, bf16...]
where the time goes in v2:
time: 86.8 us; the launch traced here: 86.4 us
  Pallas kernels  83.3 us (96%)
  local copies, waits for them, and re-layouts  3.1 us (4%)
    pallas_call x1, Pallas kernels, per_device(): pl.pallas_call(kernel, out_shape=jax.ShapeDtypeStruct(queries.shape, bf16...  83.3 us
    unnamed x1, local copies, waits for them, and re-layouts  3.1 us

profile of v2, /device:TPU:216, one launch (start us, length us, event | category | flops | bytes accessed | tf_op | source)
XLA Modules:
  0.0 86.4 jit_solution(13666856635430303543)
XLA Ops:
  0.0 83.3 %attend.1 = bf16[128,8192]{1,0:T(8,128)(2,1)} custom-call(bf16[128,8192]{1,0:T(8,128)(2,1)} %q_hbm.1, bf16[128,1024]{1,0:T(8,128)(2,1)} %k_hbm.1, bf16[128,1024]{1,0:T(8,128)(2,1)} %v_hbm.1, s32[1,64]{1,0:T(1,128)} %bitcast.1), custom_call_target="tpu_custom_call" | custom-call | tf_op jit(solution)/shard_map/attend/pallas_call | solution.py:341
  83.3 3.1 %copy.6 = bf16[128,8192]{1,0:T(8,128)(2,1)} copy(bf16[128,8192]{1,0:T(8,128)(2,1)} %attend.1) | data formatting | bytes 4194304

commit v3 on v2

--- a/solution.py
+++ b/solution.py
@@ -107,40 +107,38 @@
         to_right, to_left = full, full
         if part is not None:
             if row == 0:
-                to_right, to_left = full | part & (x < 3), full | part & (x == 0)
+                to_right, to_left = full | part & (x < 3), full | part & (x <= t)
             else:
-                to_right, to_left = full | part & (x == 3), full | part & (x > 0)
+                to_right, to_left = full | part & (x >= 2 + t), full | part & (x > 0)
         here = (row, slot, t)
         source = here if source is None else source
         send(to_right, source, here, ss_x.at[phase, t], p.right)
         send(to_left, source, here, ss_x.at[phase, 2 + t], p.left)
         send(gathers, source, (1, slot, t), ss_c.at[slot, t], p.twin)
 
-    def middle(phase, row, other):
+    def middle(phase, row, other, t):
         full, part, gathers = modes(row, other)
         base = p.other if other else p.own
         sl, sr = base + p.xl, base + p.xr
         inner = (x == 1) | (x == 2)
-        from_left, from_right = full, full
-        on_right, on_left = [full, None], [None, full]
+        from_left, from_right, hand_on = full, full, full
         if part is not None:
             if row == 0:
-                from_left, from_right = full | part & (x > 0), full | part & (x == 3)
-                on_right = [full | part & inner, part & inner]
+                from_left, from_right = full | part & (x > 0), full | part & ((x == 3) | (x == 0) & (t == 1))
+                hand_on = full | part & (inner if t == 0 else ~inner)
             else:
-                from_left, from_right = full | part & (x == 0), full | part & (x < 3)
-                on_left = [part & inner, full | part & inner]
-        for t in range(2):
-            here = (row, sl, t)
-            arrived(from_left, here)
-            if on_right[t] is not None:
-                send(on_right[t], here, here, ss_x.at[phase, 4 + t], p.right)
-            send(gathers, here, (1, sl, t), ss_c.at[sl, t], p.twin)
-            here = (row, sr, t)
-            arrived(from_right, here)
-            if on_left[t] is not None:
-                send(on_left[t], here, here, ss_x.at[phase, 6 + t], p.left)
-            send(gathers, here, (1, sr, t), ss_c.at[sr, t], p.twin)
+                from_left, from_right = full | part & ((x == 0) | (x == 3) & (t == 0)), full | part & (x < 3)
+                hand_on = full | part & (~inner if t == 0 else inner)
+        here = (row, sl, t)
+        arrived(from_left, here)
+        if t == 0:
+            send(hand_on, here, here, ss_x.at[phase, 4], p.right)
+        send(gathers, here, (1, sl, t), ss_c.at[sl, t], p.twin)
+        here = (row, sr, t)
+        arrived(from_right, here)
+        if t == 1:
+            send(hand_on, here, here, ss_x.at[phase, 5], p.left)
+        send(gathers, here, (1, sr, t), ss_c.at[sr, t], p.twin)
 
     def end(phase, row, other):
         full, part, gathers = modes(row, other)
@@ -152,11 +150,6 @@
             here = (row, so, t)
             arrived(got, here)
             send(gathers, here, (1, so, t), ss_c.at[so, t], p.twin)
-
-    def twin_sent(slots):
-        for slot in slots:
-            for t in range(2):
-                arrived(s >= 1, (1, slot, t))
 
     def block_mask(row, slot):
         pos = ((s - row) * 8 + slot) * TOK + lax.broadcasted_iota(jnp.int32, (TOK, DH), 0)
@@ -220,13 +213,13 @@
 
     far = p.other + x
     wanted = (core == 1) | (p.z == 0)
+    passes = [((core == 1) & (p.z == 1)) | ((p.z == 0) & ((p.y != 3) | (t == 1) & (s < 8))) for t in range(2)]
     mine = (k_hbm, v_hbm)
     for t in range(2):
         send(p.has_later, mine[t], (2, h, t), ss_y.at[0, t], p.later)
         begin(0, 0, False, t, mine[t])
-    crosses = p.y == 3
-    exchange = [send(None, mine[t], (0, h, t), ss_z.at[t], p.far, p.y != 3) for t in range(2)]
-
+    for t in range(2):
+        send(None, mine[t], (0, h, t), ss_z.at[t], p.far)
 
     lens = jnp.concatenate([len_ref[...], jnp.zeros((1, DH - len_ref.shape[1]), jnp.int32)], axis=1)
     lens = jnp.broadcast_to(lens, (8, DH))
@@ -253,42 +246,12 @@
     loads[1].wait()
     attend([(0, h)], first=True)
 
-    @pl.when(crosses)
-    def _():
-        for t in range(2):
-            when(p.has_later, sends[SHIFT[t]][1].wait_send)
-        for copy in exchange:
-            copy.start()
-
-    middle(0, 0, False)
-    for t in range(2):
-        arrived(p.has_before, (2, h, t))
-        begin(1, 2, False, t)
-    end(0, 0, False)
-    middle(1, 2, False)
-    for t in range(2):
-        arrived(None, (0, far, t))
-        send(p.has_later & wanted, (0, far, t), (2, far, t), ss_y.at[1, t], p.later)
-        begin(2, 0, True, t)
-    end(1, 2, False)
-
     def mixed_row(other_x):
         return jnp.where(other_x < x, 0, 2)
 
     own, other = p.own, p.other
     mixed = [(mixed_row(d), own + d) for d in (p.xl, p.xr, p.xo)] + [(2, h)]
     before = [(1, own + d) for d in range(4)]
-    attend(mixed, 0, 4)
-    attend(mixed, 4, 8)
-    middle(2, 0, True)
-    for t in range(2):
-        arrived(p.has_before & wanted, (2, far, t))
-        begin(3, 2, True, t)
-    twin_sent([own + d for d in range(4)])
-    attend(before, 0, 4)
-    end(2, 0, True)
-    attend(before, 4, 8)
-
     late_both = (core == 0) & (p.z == 0)
     row_b = jnp.where(p.z == 0, 2, 0)
     first_row = jnp.where((core == 0) & (p.z == 1), row_b, 1)
@@ -302,28 +265,72 @@
     ]
 
 
-    for t in range(2):
-        arrived(s >= 1, (1, far, t))
     early = (core == 1) & (s >= 1)
-    for d in order[1:]:
+    late = (core == 0) & (s >= 1)
+
+    def twin_sent(slot, cond):
         for t in range(2):
-            arrived(early, (1, other + d, t))
-    attend(todo[0:2])
-    middle(3, 2, True)
-    late = (core == 0) & (s >= 1)
-    for d in order[1:3]:
-        for t in range(2):
-            arrived(late, (1, other + d, t))
-    attend(todo[2:4])
-    attend(todo[4:6])
+            arrived(cond, (1, slot, t))
+
+    def from_shift(t):
+        arrived(p.has_before, (2, h, t))
+        begin(1, 2, False, t)
+        send(p.has_before & (p.y == 0) & (p.z == 1) & ((t == 0) | (s >= 16)), (2, h, t), (2, h, t), ss_z.at[2 + t], p.far)
+
+    def from_far(t):
+        arrived(None, (0, far, t))
+        send(p.has_later & passes[t], (0, far, t), (2, far, t), ss_y.at[1, t], p.later)
+        begin(2, 0, True, t)
+
+    def from_far_shift(t):
+        arrived(p.has_before & wanted, (2, far, t))
+        begin(3, 2, True, t)
+
+    def row_before(lo, hi):
+        if lo == 0:
+            for d in range(4):
+                twin_sent(own + d, s >= 1)
+        attend(before, lo, hi)
+
+    def left_over(i):
+        if i == 0:
+            twin_sent(far, s >= 1)
+            for d in order[1:]:
+                twin_sent(other + d, early)
+        if i == 1:
+            for d in order[1:3]:
+                twin_sent(other + d, late)
+        if i == 3:
+            twin_sent(other + p.xo, late)
+        attend(todo[2 * i:2 * i + 2], last=i == 3)
+
+    middle(0, 0, False, 0)
+    from_shift(0)
+    middle(0, 0, False, 1)
+    from_shift(1)
+    end(0, 0, False)
+    middle(1, 2, False, 0)
+    from_far(0)
+    middle(1, 2, False, 1)
+    from_far(1)
+    end(1, 2, False)
+    attend(mixed, 0, 4)
+    middle(2, 0, True, 0)
+    middle(2, 0, True, 1)
+    from_far_shift(0)
+    from_far_shift(1)
+    attend(mixed, 4, 8)
+    row_before(0, 4)
+    end(2, 0, True)
+    row_before(4, 8)
+    left_over(0)
+    middle(3, 2, True, 0)
+    middle(3, 2, True, 1)
+    left_over(1)
+    left_over(2)
     end(3, 2, True)
-    for t in range(2):
-        arrived(late, (1, other + p.xo, t))
-    attend(todo[6:8], last=True)
-
-    for i, (cond, copy) in enumerate(sends):
-        if i in SHIFT:
-            cond = cond & jnp.logical_not(crosses)
+    left_over(3)
+    for cond, copy in sends:
         when(cond, copy.wait_send)
     for j in range(KVH):
         columns = pl.ds(j * GROUP * DH, GROUP * DH)
@@ -332,7 +339,6 @@
 
 CHUNK = 256
 UNROLL = 4
-SHIFT = (0, 4)
 
 
 def per_device(queries, keys, values, lengths):
@@ -353,7 +359,7 @@
             pltpu.VMEM((KVH, ROWS, DH), f32),
             pltpu.VMEM((tok, H * DH), bf16),
             pltpu.VMEM((8, DH), jnp.int32),
-            dma((3,)), dma((KVH,)), dma((4, 8)), dma((8, 2)), dma((2, 2)), dma((2,)), dma((3, 8, 2)),
+            dma((3,)), dma((KVH,)), dma((4, 6)), dma((8, 2)), dma((2, 2)), dma((4,)), dma((3, 8, 2)),
         ],
         compiler_params=pltpu.CompilerParams(
             collective_id=0, has_side_effects=True, vmem_limit_bytes=56 << 20

time: 86.8 us -> 83.7 us (0.964)
  Pallas kernels: 83.3 us -> 80.5 us
    pallas_call x1, Pallas kernels: 83.3 us -> 80.5 us  [per_device(): pl.pallas_call(kernel, out_shape=jax.ShapeDtypeStruct(queries.shape, bf16...]
where the time goes in v3:
time: 83.7 us; the launch traced here: 83.6 us
  Pallas kernels  80.5 us (96%)
  local copies, waits for them, and re-layouts  3.1 us (4%)
    pallas_call x1, Pallas kernels, per_device(): pl.pallas_call(kernel, out_shape=jax.ShapeDtypeStruct(queries.shape, bf16...  80.5 us
    unnamed x1, local copies, waits for them, and re-layouts  3.1 us

profile of v3, /device:TPU:216, one launch (start us, length us, event | category | flops | bytes accessed | tf_op | source)
XLA Modules:
  0.0 83.6 jit_solution(3469521529294721658)
XLA Ops:
  0.0 80.5 %attend.1 = bf16[128,8192]{1,0:T(8,128)(2,1)} custom-call(bf16[128,8192]{1,0:T(8,128)(2,1)} %q_hbm.1, bf16[128,1024]{1,0:T(8,128)(2,1)} %k_hbm.1, bf16[128,1024]{1,0:T(8,128)(2,1)} %v_hbm.1, s32[1,64]{1,0:T(1,128)} %bitcast.1), custom_call_target="tpu_custom_call" | custom-call | tf_op jit(solution)/shard_map/attend/pallas_call | solution.py:347
  80.5 3.1 %copy.6 = bf16[128,8192]{1,0:T(8,128)(2,1)} copy(bf16[128,8192]{1,0:T(8,128)(2,1)} %attend.1) | data formatting | bytes 4194304

commit v4 on v3

--- a/solution.py
+++ b/solution.py
@@ -337,7 +337,7 @@
         pltpu.make_async_copy(out.at[:, columns], o_hbm.at[:, columns], out_sem.at[j]).wait()
 
 
-CHUNK = 256
+CHUNK = 512
 UNROLL = 4
 
 

time: 83.7 us -> 83.2 us (level)
  no operation moved by 1% of the time
where the time goes in v4:
time: 83.2 us; the launch traced here: 83.1 us
  Pallas kernels  80 us (96%)
  local copies, waits for them, and re-layouts  3.1 us (4%)
    pallas_call x1, Pallas kernels, per_device(): pl.pallas_call(kernel, out_shape=jax.ShapeDtypeStruct(queries.shape, bf16...  80 us
    unnamed x1, local copies, waits for them, and re-layouts  3.1 us

profile of v4, /device:TPU:216, one launch (start us, length us, event | category | flops | bytes accessed | tf_op | source)
XLA Modules:
  0.0 83.1 jit_solution(10990763175240043480)
XLA Ops:
  0.0 80.0 %attend.1 = bf16[128,8192]{1,0:T(8,128)(2,1)} custom-call(bf16[128,8192]{1,0:T(8,128)(2,1)} %q_hbm.1, bf16[128,1024]{1,0:T(8,128)(2,1)} %k_hbm.1, bf16[128,1024]{1,0:T(8,128)(2,1)} %v_hbm.1, s32[1,64]{1,0:T(1,128)} %bitcast.1), custom_call_target="tpu_custom_call" | custom-call | tf_op jit(solution)/shard_map/attend/pallas_call | solution.py:347
  80.0 3.1 %copy.6 = bf16[128,8192]{1,0:T(8,128)(2,1)} copy(bf16[128,8192]{1,0:T(8,128)(2,1)} %attend.1) | data formatting | bytes 4194304
